TPU v7x, 256 devices: a whole 4x4x8 slice. The times are simulated.
256 devices in a mesh: pts: 64 (over z, y_lo, x), days: 4 (over y_hi, core).
Axes of the slice: x: 4, y: 4 (y_hi: 2, y_lo: 2; y = y_hi * 2 + y_lo), z: 8, core: 2. Of those that a mesh axis runs over, the one named last changes fastest.
Arguments:
- series: bfloat16 [131072, 4096], P('pts', 'days')
- partner: int32 [64], replicated, may hold values from 0 to 63, as said below
Outputs:
- correlation: float32 [131072, 2048], P(('pts', 'days'))
- degree: float32 [131072], P(('pts', 'days'))
Inputs may be any that keep to these rules, and one draw needn't show every extreme that they name: partner pairs the 64 blocks: partner[partner[b]] = b and partner[b] != b for every block b.
All inputs are finite; a program needn't handle non-finite values.
Results may differ from a plain program's by a relative error of at most 0.00041.
Values may be sent and summed in bfloat16 or wider, within the bound.
A program may use at most 128 MiB of HBM per device.

v0:
```python
import jax
import jax.numpy as jnp
from jax import lax
from jax.sharding import PartitionSpec as P

epsilon = 1e-06


def route_partner(normed, partner):
    groups = lax.axis_size("pts")
    pieces = normed.reshape(groups, normed.shape[0] // groups, normed.shape[1])
    received = lax.all_to_all(pieces, "pts", split_axis=0, concat_axis=0, tiled=True)
    chosen = jnp.take(received, partner, axis=0)
    returned = lax.all_to_all(chosen, "pts", split_axis=0, concat_axis=0, tiled=True)
    return returned.reshape(normed.shape[0], normed.shape[1])


def contract_days(left, right):
    return lax.dot_general(
        left, right, (((1,), (1,)), ((), ())), preferred_element_type=jnp.float32
    )


def on_device(series, partner):
    shards = lax.axis_size("days")
    day_count = series.shape[1] * shards
    values = series.astype(jnp.float32)
    average = lax.psum(jnp.sum(values, axis=1), "days") / day_count
    centred = values - average[:, None]
    variance = lax.psum(jnp.sum(centred * centred, axis=1), "days") / day_count
    normed = (centred * lax.rsqrt(variance + epsilon)[:, None]).astype(jnp.bfloat16)
    other_block = route_partner(normed, partner)
    correlation = lax.psum_scatter(
        contract_days(normed, other_block) / day_count, "days", scatter_dimension=0, tiled=True
    )
    degree = jnp.sum(correlation * correlation, axis=1)
    return (correlation, degree)


def solution(mesh):
    in_specs = (P("pts", "days"), P())
    out_specs = (P(("pts", "days"), None), P(("pts", "days")))
    return jax.shard_map(
        on_device, mesh=mesh, in_specs=in_specs, out_specs=out_specs, check_vma=False
    )
```

profile of v0, /device:TPU:1, one launch (start us, length us, event | category | flops | bytes accessed | tf_op | source)
XLA Modules:
  0.0 408.7 jit_solution(14720562258553551850)
XLA Ops:
  7.2 2.8 convert_reduce_fusion
  10.0 9.8 %psum.14 = f32[2048]{0:T(1024)S(1)} all-reduce(f32[2048]{0:T(1024)S(1)} %convert_reduce_fusion), channel_id=1, replica_groups=mesh['pts'=64,'days'=4] {'days'}, use_global_device_ids=true, to_apply=%region_1.0 | all-reduce | flops 2048 | bytes 16384 | tf_op jit(solution)/shard_map/psum | solution.py:28
  19.8 3.0 fusion.2
  22.8 8.5 %psum.15 = f32[2048]{0:T(1024)S(1)} all-reduce(f32[2048]{0:T(1024)S(1)} %fusion.2), channel_id=1, replica_groups=mesh['pts'=64,'days'=4] {'days'}, use_global_device_ids=true, to_apply=%region_3.0 | all-reduce | flops 2048 | bytes 16384 | tf_op jit(solution)/shard_map/psum | solution.py:30
  31.3 4.2 %fusion.3 = bf16[2048,1024]{1,0:T(8,128)(2,1)} fusion(bf16[2048,1024]{1,0:T(8,128)(2,1)} %param.2, f32[2048]{0:T(1024)S(1)} %add_rsqrt_fusion, f32[2048]{0:T(1024)S(1)} %broadcast_multiply_fusion), kind=kLoop, calls=%fused_computation.7 | loop fusion | flops 8388608 | bytes 8404992 | tf_op jit(solution)/shard_map/convert_element_type | solution.py:31
  35.5 0.0 copy-start.1
  35.5 12.2 %all-to-all-start = ((bf16[64,32,1024]{2,1,0:T(8,128)(2,1)}), bf16[64,32,1024]{2,1,0:T(8,128)(2,1)}, u32[]{:S(2)}, u32[]{:S(2)}) async-start(bf16[64,32,1024]{2,1,0:T(8,128)(2,1)} %bitcast.4), calls=%async_computation | async-start | bytes 8388608 | tf_op jit(solution)/shard_map/all_to_all | solution.py:12
  47.7 0.0 reduce-scatter.2.cloned.1.call-start
  47.7 0.0 copy-done.1
  47.8 92.2 %all-to-all-done = bf16[64,32,1024]{2,1,0:T(8,128)(2,1)} async-done(((bf16[64,32,1024]{2,1,0:T(8,128)(2,1)}), bf16[64,32,1024]{2,1,0:T(8,128)(2,1)}, u32[]{:S(2)}, u32[]{:S(2)}) %all-to-all-start) | async-done | bytes 4194336 | tf_op jit(solution)/shard_map/all_to_all | solution.py:12
  140.0 5.0 %gather_fusion = bf16[64,32,1024]{2,1,0:T(8,128)(2,1)} fusion(bf16[64,32,1024]{2,1,0:T(8,128)(2,1)} %all-to-all-done, s32[1024]{0:T(1024)S(1)} %pad_clamp_fusion), kind=kCustom, calls=%fused_computation | custom fusion | bytes 8388864 | tf_op jit(solution)/shard_map/jit(_take)/gather | solution.py:13
  145.0 2.6 broadcast_select_fusion
  147.6 0.0 copy-start
  147.6 101.0 %all_to_all.10 = bf16[64,32,1024]{2,1,0:T(8,128)(2,1)S(1)} all-to-all(bf16[64,32,1024]{2,1,0:T(8,128)(2,1)S(1)} %broadcast_select_fusion), channel_id=1, replica_groups=mesh['pts'=64,'days'=4] {'pts'}, dimensions={0} | all-to-all | bytes 8388608 | tf_op jit(solution)/shard_map/all_to_all | solution.py:14
  248.6 0.0 copy-done
  248.6 11.7 %convolution_multiply_fusion = f32[2048,2048]{1,0:T(8,128)} fusion(bf16[2048,1024]{1,0:T(8,128)(2,1)S(1)} %copy-done, bf16[2048,1024]{1,0:T(8,128)(2,1)S(1)} %bitcast.5), kind=kOutput, calls=%fused_computation.5 | convolution fusion | flops 8594128896 | bytes 25165824 | tf_op jit(solution)/shard_map/dot_general | solution.py:19
  260.4 0.0 reduce-scatter.2.cloned.1.call-update
  260.4 138.3 %reduce-scatter.2.cloned.1.call-done = f32[512,2048]{1,0:T(8,128)} async-done(((f32[2048,2048]{1,0:T(8,128)}), f32[512,2048]{1,0:T(8,128)}) %reduce-scatter.2.cloned.1.call-update) | async-done | bytes 4194320 | tf_op jit(solution)/shard_map/reduce_scatter | solution.py:33
  398.7 3.1 multiply_reduce_fusion
  (5 shorter events, 0.0 us)
Async XLA Ops:
  35.5 12.2 %copy-start.1 = (s32[64]{0:T(128)S(1)}, s32[64]{0:T(128)}, u32[]{:S(2)}) copy-start(s32[64]{0:T(128)} %param.3) | copy-start | bytes 772
  35.5 104.5 %all-to-all-start = ((bf16[64,32,1024]{2,1,0:T(8,128)(2,1)}), bf16[64,32,1024]{2,1,0:T(8,128)(2,1)}, u32[]{:S(2)}, u32[]{:S(2)}) async-start(bf16[64,32,1024]{2,1,0:T(8,128)(2,1)} %bitcast.4), calls=%async_computation | async-start | bytes 8388608 | tf_op jit(solution)/shard_map/all_to_all | solution.py:12
  47.7 351.0 %reduce-scatter.2.cloned.1.call-start = ((), (), s32[]{:S(2)}) async-start(), calls=%async_computation.3 | async-start | bytes 20971520 | tf_op jit(solution)/shard_map/reduce_scatter | solution.py:33
  147.6 101.1 %copy-start = (bf16[2048,1024]{1,0:T(8,128)(2,1)S(1)}, bf16[2048,1024]{1,0:T(8,128)(2,1)}, u32[]{:S(2)}) copy-start(bf16[2048,1024]{1,0:T(8,128)(2,1)} %fusion.3) | copy-start | bytes 12582916
Sparse Core Ops, SparseCore 0:
  260.5 138.1 reduce-scatter.1
where the time goes:
time: 409 us
  waiting for transfers between devices  231 us (56%)
  blocking collectives  119 us (29%)
  other arithmetic  15.7 us (4%)
  between operations  14.1 us (3%)
  starting transfers between devices  12.2 us (3%)
  matrix products  11.7 us (3%)
  local copies, waits for them, and re-layouts  4.98 us (1%)
    reduce_scatter x1, waiting for transfers between devices, on_device(): lax.psum_scatter(contract_days(normed, other_block) / day_count, 'days',...  138 us
    all_to_all x1, blocking collectives, route_partner(): lax.all_to_all(chosen, 'pts', split_axis=0, concat_axis=0, tiled=True)  101 us
    all_to_all x1, waiting for transfers between devices, route_partner(): lax.all_to_all(pieces, 'pts', split_axis=0, concat_axis=0, tiled=True)  92.2 us
    all_to_all x1, starting transfers between devices, route_partner(): lax.all_to_all(pieces, 'pts', split_axis=0, concat_axis=0, tiled=True)  12.2 us
    dot_general x1, matrix products, contract_days(): lax.dot_general(left, right, (((1,), (1,)), ((), ())), preferred_element_...  11.7 us
    psum x1, blocking collectives, on_device(): average = lax.psum(jnp.sum(values, axis=1), 'days') / day_count  9.83 us
    psum x1, blocking collectives, on_device(): variance = lax.psum(jnp.sum(centred * centred, axis=1), 'days') / day_count  8.52 us
  transfers between devices with their start and end apart: 2, of which 2 were waited for; matrix products, arithmetic and copies ran while one was open for 0% of the time, Pallas kernels for 0%

commit v1 on v0

v1 whole, which is shorter than its diff:
```python
import functools

import jax
import jax.numpy as jnp
from jax import lax
from jax.experimental import pallas as pl
from jax.experimental.pallas import tpu as pltpu
from jax.sharding import Mesh, PartitionSpec as P

epsilon = 1e-06

PTS = ("z", "yl", "x")
DAYS = ("yh", "core")
FIRST_PARTS = 2
CHUNKS = 4
MESH = pl.DeviceIdType.MESH


def remote(src, dst, send, recv, **device):
    return pltpu.make_async_remote_copy(
        src_ref=src, dst_ref=dst, send_sem=send, recv_sem=recv, device_id=device, device_id_type=MESH
    )


def wait_bytes(ref, sem):
    pltpu.make_async_copy(ref, ref, sem).wait()


def kernel(
    sizes,
    partner,
    series,
    out,
    stats,
    final,
    normed,
    inboxes,
    chosen,
    landed,
    own,
    full,
    stat_send,
    stat_recv,
    own_send,
    own_recv,
    first_send,
    first_recv,
    second_send,
    second_recv,
    y_send,
    y_recv,
    core_send,
    core_recv,
):
    Z, YL, X, YH, C = sizes
    z, yl, x, yh, core = (lax.axis_index(name) for name in PTS + DAYS)
    groups = Z * YL * X
    flat = Z * X
    quarters = YH * C
    points, days = series.shape
    piece = points // groups
    rows = points // quarters
    width = days // FIRST_PARTS
    span = days // CHUNKS
    block = (z * YL + yl) * X + x
    zx = z * X + x
    day = yh * C + core
    here = yl * quarters + day

    def peer(o):
        return (
            lax.rem(z + lax.rem(o * 3, Z), Z),
            lax.rem(yl + lax.rem(o // Z, YL), YL),
            lax.rem(x + o // (Z * YL), X),
        )

    def other_day(o):
        to = lax.rem(day + o, quarters)
        return to, lax.div(to, C), lax.rem(to, C)

    barrier = pltpu.get_barrier_semaphore()

    def greet(o, carry):
        pz, py, px = peer(o)
        pl.semaphore_signal(barrier, inc=1, device_id={"z": pz, "yl": py, "x": px}, device_id_type=MESH)
        return carry

    lax.fori_loop(1, groups, greet, 0)
    for o in range(1, quarters):
        _, ph, pc = other_day(o)
        pl.semaphore_signal(barrier, inc=1, device_id={"yh": ph, "core": pc}, device_id_type=MESH)
    pl.semaphore_signal(barrier, inc=1, device_id={"yl": 1 - yl, "yh": 1 - yh}, device_id_type=MESH)

    tile = 128
    eye = lax.broadcasted_iota(jnp.int32, (tile, tile), 0) == lax.broadcasted_iota(jnp.int32, (tile, tile), 1)

    def to_lanes(column):
        return jnp.sum(jnp.where(eye, column, 0.0), axis=0, keepdims=True)

    def to_rows(line):
        return jnp.sum(jnp.where(eye, line, 0.0), axis=1, keepdims=True)

    def local_stats(g, carry):
        values = series[pl.ds(pl.multiple_of(g * tile, tile), tile), :].astype(jnp.float32)
        mean = jnp.sum(values, axis=1, keepdims=True) / days
        centred = values - mean
        squares = jnp.sum(centred * centred, axis=1, keepdims=True)
        stats[day, 0, pl.ds(g, 1), :] = to_lanes(mean)
        stats[day, 1, pl.ds(g, 1), :] = to_lanes(squares)
        return carry

    lax.fori_loop(0, points // tile, local_stats, 0)

    pl.semaphore_wait(barrier, groups - 1 + quarters - 1 + 1)

    for o in range(1, quarters):
        _, ph, pc = other_day(o)
        remote(stats.at[day], stats.at[day], stat_send, stat_recv.at[o - 1], yh=ph, core=pc).start()
    for o in range(1, quarters):
        wait_bytes(stats.at[0], stat_recv.at[o - 1])

    means = [stats[d, 0] for d in range(quarters)]
    average = sum(means) / quarters
    spread = sum(stats[d, 1] for d in range(quarters))
    spread += days * sum((m - average) * (m - average) for m in means)
    final[0] = average
    final[1] = lax.rsqrt(spread / (days * quarters) + epsilon)

    def normalise(g, carry):
        at = pl.ds(pl.multiple_of(g * tile, tile), tile)
        values = series[at, :].astype(jnp.float32)
        centred = values - to_rows(final[0, pl.ds(g, 1), :])
        normed[at, :] = (centred * to_rows(final[1, pl.ds(g, 1), :])).astype(jnp.bfloat16)
        return carry

    lax.fori_loop(0, points // tile, normalise, 0)

    def first_part(part):
        cols = pl.ds(part * width, width)

        def send(o, carry):
            pz, py, px = peer(o)
            to = py * flat + pz * X + px
            remote(
                normed.at[pl.ds(pl.multiple_of(to * piece, piece), piece), cols],
                inboxes[part].at[block],
                first_send,
                first_recv.at[part],
                z=pz,
                yl=py,
                x=px,
            ).start()
            return carry

        lax.fori_loop(1, groups, send, 0)

    first_part(0)
    for o in range(1, quarters):
        to, ph, pc = other_day(o)
        remote(
            normed.at[pl.ds(pl.multiple_of(to * rows, rows), rows), :],
            own.at[day],
            own_send,
            own_recv,
            yh=ph,
            core=pc,
        ).start()
    for part in range(1, FIRST_PARTS):
        first_part(part)
    mine = yl * flat + zx
    for part in range(FIRST_PARTS):
        cols = pl.ds(part * width, width)
        inboxes[part][block] = normed[pl.ds(pl.multiple_of(mine * piece, piece), piece), cols]
    own[day] = normed[pl.ds(pl.multiple_of(day * rows, rows), rows), :]

    def second_hop(k):
        inbox = inboxes[k * span // width]
        cols = pl.ds(k * span % width, span)

        def pick(t, carry):
            to_z, to_y, to_x = t // (YL * X), lax.rem(t // X, YL), lax.rem(t, X)
            chosen[k, to_z * X + to_x, to_y] = inbox[partner[t], :, cols]
            return carry

        lax.fori_loop(0, groups, pick, 0)
        for half in range(YL):
            landed[k, half, zx] = chosen[k, zx, half]

        def send(o, carry):
            pz = lax.rem(z + lax.rem(o * 3, Z), Z)
            px = lax.rem(x + o // Z, X)
            remote(
                chosen.at[k, pz * X + px],
                landed.at[k, :, zx],
                second_send,
                second_recv.at[k],
                z=pz,
                x=px,
            ).start()
            return carry

        lax.fori_loop(1, flat, send, 0)

    def y_source(j):
        if j == 0:
            return yl * quarters + (1 - yh) * C + core
        return (1 - yl) * quarters + (j - 1) * C + core

    def spread_y(k):
        wait_bytes(chosen.at[k, pl.ds(0, flat - 1)], second_recv.at[k])
        remote(
            landed.at[k, yl], full.at[k, here], y_send, y_recv.at[k, 0], yh=1 - yh
        ).start()
        for to in range(YH):
            remote(
                landed.at[k, 1 - yl], full.at[k, here], y_send, y_recv.at[k, 1 + yh], yl=1 - yl, yh=to
            ).start()
        remote(landed.at[k, yl], full.at[k, here], core_send, core_recv.at[k], core=1 - core).start()
        full[k, here] = landed[k, yl]

    def spread_core(k):
        for j in range(3):
            wait_bytes(full.at[k, 0], y_recv.at[k, j])
            at = y_source(j)
            remote(full.at[k, at], full.at[k, at], core_send, core_recv.at[k], core=1 - core).start()

    columns = min(256, flat * piece)
    tiles = flat * piece // columns

    def multiply(k):
        wait_bytes(full.at[k, pl.ds(0, 4)], core_recv.at[k])

        def one(n, carry):
            half, t = n // tiles, lax.rem(n, tiles)
            group = columns // piece
            total = None
            for q in range(quarters):
                right = full[k, half * quarters + q, pl.ds(t * group, group)].reshape(columns, span)
                term = lax.dot_general(
                    own[q, :, pl.ds(k * span, span)],
                    right,
                    (((1,), (1,)), ((), ())),
                    preferred_element_type=jnp.float32,
                )
                total = term if total is None else total + term
            at = pl.ds(pl.multiple_of(n * columns, columns), columns)
            out[:, at] = total if k == 0 else out[:, at] + total
            return carry

        lax.fori_loop(0, YL * tiles, one, 0)

    ahead = 1
    for step in range(CHUNKS + ahead + 2):
        if step < CHUNKS:
            if step * span % width == 0:
                part = step * span // width
                wait_bytes(inboxes[part].at[pl.ds(0, groups - 1)], first_recv.at[part])
            second_hop(step)
        k = step - ahead
        if 0 <= k < CHUNKS:
            spread_y(k)
        k = step - ahead - 1
        if 0 <= k < CHUNKS:
            spread_core(k)
        k = step - ahead - 2
        if 0 <= k < CHUNKS:
            if k == 0:
                wait_bytes(own.at[pl.ds(0, quarters - 1)], own_recv)
            multiply(k)

    wait_bytes(stats.at[pl.ds(0, quarters - 1)], stat_send)
    wait_bytes(own.at[pl.ds(0, quarters - 1)], own_send)
    wait_bytes(normed.at[pl.ds(0, (groups - 1) * piece)], first_send)
    wait_bytes(chosen.at[:, pl.ds(0, flat - 1)], second_send)
    wait_bytes(full.at[:, pl.ds(0, 3)], y_send)
    wait_bytes(full.at[:, pl.ds(0, 4)], core_send)


def on_device(sizes, series, partner):
    Z, YL, X, YH, C = sizes
    groups, flat, quarters = Z * YL * X, Z * X, YH * C
    points, days = series.shape
    piece, rows, span = points // groups, points // quarters, days // CHUNKS
    bf16 = jnp.bfloat16
    dma = pltpu.SemaphoreType.DMA
    total = pl.pallas_call(
        functools.partial(kernel, sizes),
        out_shape=jax.ShapeDtypeStruct((rows, points), jnp.float32),
        in_specs=[
            pl.BlockSpec(memory_space=pltpu.SMEM),
            pl.BlockSpec(memory_space=pltpu.VMEM),
        ],
        out_specs=pl.BlockSpec(memory_space=pltpu.VMEM),
        scratch_shapes=[
            pltpu.VMEM((quarters, 2, points // 128, 128), jnp.float32),
            pltpu.VMEM((2, points // 128, 128), jnp.float32),
            pltpu.VMEM((points, days), bf16),
            [pltpu.VMEM((groups, piece, days // FIRST_PARTS), bf16) for _ in range(FIRST_PARTS)],
            pltpu.VMEM((CHUNKS, flat, YL, piece, span), bf16),
            pltpu.VMEM((CHUNKS, YL, flat, piece, span), bf16),
            pltpu.VMEM((quarters, rows, days), bf16),
            pltpu.VMEM((CHUNKS, YL * quarters, flat, piece, span), bf16),
            dma,
            dma((quarters - 1,)),
            dma,
            dma,
            dma,
            dma((FIRST_PARTS,)),
            dma,
            dma((CHUNKS,)),
            dma,
            dma((CHUNKS, 3)),
            dma,
            dma((CHUNKS,)),
        ],
        compiler_params=pltpu.CompilerParams(
            collective_id=0, has_side_effects=True, vmem_limit_bytes=58 * 2**20
        ),
        cost_estimate=pl.CostEstimate(
            flops=2 * rows * points * days * quarters, bytes_accessed=12 * 2**20, transcendentals=0
        ),
    )(partner, series)
    correlation = total * (1.0 / (days * quarters))
    degree = jnp.sum(correlation * correlation, axis=1)
    return (correlation, degree)


def solution(mesh):
    sizes = (8, 2, 4, 2, 2)
    fine = Mesh(mesh.devices.reshape(sizes), PTS + DAYS)
    in_specs = (P(PTS, DAYS), P())
    out_specs = (P(PTS + DAYS, None), P(PTS + DAYS))
    return jax.shard_map(
        functools.partial(on_device, sizes), mesh=fine, in_specs=in_specs, out_specs=out_specs, check_vma=False
    )
```

time: 409 us -> 244 us (0.60)
  Pallas kernels: 0 us -> 238 us
  waiting for transfers between devices: 231 us -> 0 us
  blocking collectives: 119 us -> 0 us
  between operations: 14.1 us -> 0.64 us
  starting transfers between devices: 12.2 us -> 0 us
  matrix products: 11.7 us -> 0 us
  other arithmetic: 15.7 us -> 5.17 us
  local copies, waits for them, and re-layouts: 4.98 us -> 0 us
    pallas_call x0 -> x1, Pallas kernels: none -> 238 us  [on_device(): pl.pallas_call(functools.partial(kernel, sizes), out_shape=jax.ShapeDtype...]
    reduce_scatter x1 -> x0, waiting for transfers between devices: 138 us -> none  [on_device(): lax.psum_scatter(contract_days(normed, other_block) / day_count, 'days',...]
    all_to_all x1 -> x0, blocking collectives: 101 us -> none  [route_partner(): lax.all_to_all(chosen, 'pts', split_axis=0, concat_axis=0, tiled=True)]
    all_to_all x1 -> x0, waiting for transfers between devices: 92.2 us -> none  [route_partner(): lax.all_to_all(pieces, 'pts', split_axis=0, concat_axis=0, tiled=True)]
    psum x2 -> x0, blocking collectives: 18.3 us -> none  [the longest x1 9.83 us: on_device(): average = lax.psum(jnp.sum(values, axis=1), 'days') / day_count]
    all_to_all x1 -> x0, starting transfers between devices: 12.2 us -> none  [route_partner(): lax.all_to_all(pieces, 'pts', split_axis=0, concat_axis=0, tiled=True)]
    dot_general x1 -> x0, matrix products: 11.7 us -> none  [contract_days(): lax.dot_general(left, right, (((1,), (1,)), ((), ())), preferred_element_...]
    reduce_sum x2 -> x0, other arithmetic: 5.78 us -> none  [the longest x1 2.98 us: on_device(): variance = lax.psum(jnp.sum(centred * centred, axis=1), 'days') / day_count]
  transfers between devices with their start and end apart: 2 -> 0, of which waited for: 2 -> 0; matrix products, arithmetic and copies ran while one was open for 0% -> 0% of each run, Pallas kernels for 0% -> 0%
where the time goes in v1:
time: 244 us
  Pallas kernels  238 us (98%)
  other arithmetic  5.17 us (2%)
    pallas_call x1, Pallas kernels, on_device(): pl.pallas_call(functools.partial(kernel, sizes), out_shape=jax.ShapeDtype...  238 us
    reduce_sum x1, other arithmetic, on_device(): degree = jnp.sum(correlation * correlation, axis=1)  5.17 us

profile of v1, /device:TPU:1, one launch (start us, length us, event | category | flops | bytes accessed | tf_op | source)
XLA Modules:
  0.0 244.0 jit_solution(16340227213420315451)
XLA Ops:
  0.6 238.2 %shard_map.41 = f32[512,2048]{1,0:T(8,128)} custom-call(s32[64]{0:T(128)} %partner.1, bf16[2048,1024]{1,0:T(8,128)(2,1)} %series.1), custom_call_target="tpu_custom_call" | custom-call | flops 8589934592 | bytes 12582912 | tf_op jit(solution)/shard_map/pallas_call | solution.py:286
  238.8 5.2 %multiply_reduce_fusion = (f32[512]{0:T(512)}, f32[512,2048]{1,0:T(8,128)}) fusion(f32[512,2048]{1,0:T(8,128)} %shard_map.41), kind=kLoop, calls=%fused_computation | loop fusion | flops 3145216 | bytes 8390656 | tf_op jit(solution)/shard_map/reduce_sum | solution.py:324

commit v2 on v1

v2 whole, which is shorter than its diff:
```python
import functools

import jax
import jax.numpy as jnp
from jax import lax
from jax.experimental import pallas as pl
from jax.experimental.pallas import tpu as pltpu
from jax.sharding import Mesh, PartitionSpec as P

epsilon = 1e-06

PTS = ("z", "yl", "x")
DAYS = ("yh", "core")
FIRST_PARTS = 4
CHUNKS = 8
AHEAD = 3
LAG = 2
MESH = pl.DeviceIdType.MESH


def remote(src, dst, send, recv, **device):
    return pltpu.make_async_remote_copy(
        src_ref=src, dst_ref=dst, send_sem=send, recv_sem=recv, device_id=device, device_id_type=MESH
    )


def wait_bytes(ref, sem):
    pltpu.make_async_copy(ref, ref, sem).wait()


def kernel(
    sizes,
    partner,
    series,
    out,
    local,
    stats,
    final,
    scales,
    shift,
    factor,
    inboxes,
    chosen,
    landed,
    own,
    full,
    gate,
    local_sem,
    stat_send,
    stat_recv,
    scale_send,
    scale_recv,
    own_send,
    own_recv,
    first_send,
    first_recv,
    second_send,
    second_recv,
    y_send,
    y_recv,
    core_send,
    core_recv,
):
    Z, YL, X, YH, C = sizes
    z, yl, x, yh, core = (lax.axis_index(name) for name in PTS + DAYS)
    groups = Z * YL * X
    flat = Z * X
    quarters = YH * C
    points, days = series.shape
    piece = points // groups
    rows = points // quarters
    width = days // FIRST_PARTS
    span = days // CHUNKS
    block = (z * YL + yl) * X + x
    zx = z * X + x
    mine = yl * flat + zx
    day = yh * C + core
    here = yl * quarters + day
    tile = 128
    per_tile = tile // piece

    def peer(o):
        return (
            lax.rem(z + lax.rem(o * 3, Z), Z),
            lax.rem(yl + lax.rem(o // Z, YL), YL),
            lax.rem(x + o // (Z * YL), X),
        )

    def other_day(o):
        to = lax.rem(day + o, quarters)
        return to, lax.div(to, C), lax.rem(to, C)

    barrier = pltpu.get_barrier_semaphore()
    plane = YL * X

    def plane_peer(o):
        return {"yl": lax.rem(yl + o // X, YL), "x": lax.rem(x + o % X, X)}

    for o in range(1, plane):
        pl.semaphore_signal(barrier, inc=1, device_id=plane_peer(o), device_id_type=MESH)
    for o in range(1, Z):
        pl.semaphore_signal(barrier, inc=1, device_id={"z": lax.rem(z + o, Z)}, device_id_type=MESH)
    for o in range(1, quarters):
        _, ph, pc = other_day(o)
        pl.semaphore_signal(barrier, inc=1, device_id={"yh": ph, "core": pc}, device_id_type=MESH)
    pl.semaphore_signal(barrier, inc=1, device_id={"yl": 1 - yl, "yh": 1 - yh}, device_id_type=MESH)
    local_copy = pltpu.make_async_copy(series, local, local_sem)
    local_copy.start()
    pl.semaphore_wait(barrier, plane - 1 + Z - 1 + quarters - 1 + 1)
    for o in range(1, plane):
        pl.semaphore_signal(gate, inc=1, device_id=plane_peer(o), device_id_type=MESH)
    pl.semaphore_wait(gate, plane - 1)

    def first_part(part):
        cols = pl.ds(part * width, width)

        def send(o, carry):
            pz, py, px = peer(o)
            to = py * flat + pz * X + px
            remote(
                series.at[pl.ds(pl.multiple_of(to * piece, piece), piece), cols],
                inboxes[part].at[block],
                first_send,
                first_recv.at[part],
                z=pz,
                yl=py,
                x=px,
            ).start()
            return carry

        lax.fori_loop(1, groups, send, 0)

    first_part(0)
    local_copy.wait()

    eye = lax.broadcasted_iota(jnp.int32, (tile, tile), 0) == lax.broadcasted_iota(jnp.int32, (tile, tile), 1)

    def to_lanes(column):
        return jnp.sum(jnp.where(eye, column, 0.0), axis=0, keepdims=True)

    def to_rows(line):
        return jnp.sum(jnp.where(eye, line, 0.0), axis=1, keepdims=True)

    def local_stats(g, carry):
        values = local[pl.ds(pl.multiple_of(g * tile, tile), tile), :].astype(jnp.float32)
        mean = jnp.sum(values, axis=1, keepdims=True) / days
        centred = values - mean
        squares = jnp.sum(centred * centred, axis=1, keepdims=True)
        stats[day, g, pl.ds(0, 1), :] = to_lanes(mean)
        stats[day, g, pl.ds(1, 1), :] = to_lanes(squares)
        return carry

    lax.fori_loop(0, points // tile, local_stats, 0)
    for o in range(1, quarters):
        _, ph, pc = other_day(o)
        remote(stats.at[day], stats.at[day], stat_send, stat_recv.at[o - 1], yh=ph, core=pc).start()
    if FIRST_PARTS > 1:
        first_part(1)
    for o in range(1, quarters):
        wait_bytes(stats.at[0], stat_recv.at[o - 1])

    def whole_stats(g, carry):
        means = [stats[d, g, pl.ds(0, 1), :] for d in range(quarters)]
        average = sum(means) / quarters
        spread = sum(stats[d, g, pl.ds(1, 1), :] for d in range(quarters))
        spread += days * sum((m - average) * (m - average) for m in means)
        final[g, pl.ds(0, 1), :] = average
        final[g, pl.ds(1, 1), :] = lax.rsqrt(spread / (days * quarters) + epsilon)
        return carry

    lax.fori_loop(0, points // tile, whole_stats, 0)

    def send_scale(o, carry):
        pz, py, px = peer(o)
        to = py * flat + pz * X + px
        remote(
            final.at[to // per_tile], scales.at[block], scale_send, scale_recv, z=pz, yl=py, x=px
        ).start()
        return carry

    lax.fori_loop(1, groups, send_scale, 0)
    for o in range(1, quarters):
        to, ph, pc = other_day(o)
        remote(
            series.at[pl.ds(pl.multiple_of(to * rows, rows), rows), :],
            own.at[day],
            own_send,
            own_recv,
            yh=ph,
            core=pc,
        ).start()
    for part in range(2, FIRST_PARTS):
        first_part(part)
    for part in range(FIRST_PARTS):
        cols = pl.ds(part * width, width)
        inboxes[part][block] = local[pl.ds(pl.multiple_of(mine * piece, piece), piece), cols]
    own[day] = local[pl.ds(pl.multiple_of(day * rows, rows), rows), :]
    scales[block] = final[mine // per_tile]

    wait_bytes(scales.at[pl.ds(0, groups - 1)], scale_recv)
    lane = lax.broadcasted_iota(jnp.int32, (piece, tile), 1)
    line = lax.broadcasted_iota(jnp.int32, (piece, tile), 0) + lax.rem(mine, per_tile) * piece
    at_lane = lane == line

    def expand(b, carry):
        for which, to in ((0, shift), (1, factor)):
            column = jnp.sum(jnp.where(at_lane, scales[b, pl.ds(which, 1), :], 0.0), axis=1, keepdims=True)
            to[b] = jnp.broadcast_to(column, (piece, tile))
        return carry

    lax.fori_loop(0, groups, expand, 0)

    def normalise_own():
        def one(g, carry):
            at = pl.ds(pl.multiple_of(g * tile, tile), tile)
            average = to_rows(final[day * (rows // tile) + g, pl.ds(0, 1), :])
            scale = to_rows(final[day * (rows // tile) + g, pl.ds(1, 1), :])
            for q in range(quarters):
                values = own[q, at, :].astype(jnp.float32)
                own[q, at, :] = ((values - average) * scale).astype(jnp.bfloat16)
            return carry

        lax.fori_loop(0, rows // tile, one, 0)

    def half_of(unit):
        return 1 - yl if unit % 2 else yl

    def second_hop(unit):
        k, half = unit // 2, half_of(unit)
        inbox = inboxes[k * span // width]

        def pick(t, carry):
            source = partner[(t // X * YL + half) * X + lax.rem(t, X)]
            for j in range(0, span, tile):
                values = inbox[source, :, pl.ds(k * span % width + j, tile)].astype(jnp.float32)
                values = (values - shift[source]) * factor[source]
                chosen[k, half, t, :, pl.ds(j, tile)] = values.astype(jnp.bfloat16)
            return carry

        lax.fori_loop(0, flat, pick, 0)
        landed[k, half, zx] = chosen[k, half, zx]

        def send(o, carry):
            pz = lax.rem(z + lax.rem(o * 3, Z), Z)
            px = lax.rem(x + o // Z, X)
            remote(
                chosen.at[k, half, pz * X + px],
                landed.at[k, half, zx],
                second_send,
                second_recv.at[unit],
                z=pz,
                x=px,
            ).start()
            return carry

        lax.fori_loop(1, flat, send, 0)

    def spread_y(unit):
        k, half = unit // 2, half_of(unit)
        wait_bytes(chosen.at[k, 0, pl.ds(0, flat - 1)], second_recv.at[unit])
        if unit % 2 == 0:
            remote(landed.at[k, half], full.at[k, here], y_send, y_recv.at[k, 0], yh=1 - yh).start()
            remote(landed.at[k, half], full.at[k, here], core_send, core_recv.at[k], core=1 - core).start()
            full[k, here] = landed[k, half]
        else:
            for to in range(YH):
                remote(
                    landed.at[k, half], full.at[k, here], y_send, y_recv.at[k, 1 + yh], yl=1 - yl, yh=to
                ).start()

    def spread_core(unit):
        k = unit // 2
        if unit % 2 == 0:
            arrivals = [(0, yl * quarters + (1 - yh) * C + core)]
        else:
            arrivals = [(1 + h, (1 - yl) * quarters + h * C + core) for h in range(YH)]
        for j, at in arrivals:
            wait_bytes(full.at[k, 0], y_recv.at[k, j])
            remote(full.at[k, at], full.at[k, at], core_send, core_recv.at[k], core=1 - core).start()

    columns = min(256, flat * piece)
    tiles = flat * piece // columns

    def multiply(k, cores):
        quarter = [h * C + c for c in cores for h in range(YH)]
        group = columns // piece

        def one(n, carry):
            half, t = n // tiles, lax.rem(n, tiles)
            left = jnp.concatenate([own[q, :, pl.ds(k * span, span)] for q in quarter], axis=1)
            right = jnp.concatenate(
                [
                    full[k, half * quarters + q, pl.ds(t * group, group)].reshape(columns, span)
                    for q in quarter
                ],
                axis=1,
            )
            total = lax.dot_general(left, right, (((1,), (1,)), ((), ())), preferred_element_type=jnp.float32)
            at = pl.ds(pl.multiple_of(n * columns, columns), columns)
            out[:, at] = total if k == 0 else out[:, at] + total
            return carry

        lax.fori_loop(0, YL * tiles, one, 0)

    units = 2 * CHUNKS
    for step in range(units + AHEAD + LAG + 1):
        if step < units:
            if step // 2 * span % width == 0 and step % 2 == 0:
                part = step // 2 * span // width
                wait_bytes(inboxes[part].at[pl.ds(0, groups - 1)], first_recv.at[part])
            second_hop(step)
        unit = step - AHEAD
        if 0 <= unit < units:
            spread_y(unit)
        unit = step - AHEAD - LAG
        if 0 <= unit < units:
            spread_core(unit)
        unit = step - AHEAD - LAG - 1
        if unit > 0 and unit % 2:
            k = unit // 2
            if k == 0:
                wait_bytes(own.at[pl.ds(0, quarters - 1)], own_recv)
                normalise_own()
            if k == CHUNKS - 1:
                multiply(k, [core])
            wait_bytes(full.at[k, pl.ds(0, 4)], core_recv.at[k])
            multiply(k, [1 - core] if k == CHUNKS - 1 else range(C))

    wait_bytes(stats.at[pl.ds(0, quarters - 1)], stat_send)
    wait_bytes(own.at[pl.ds(0, quarters - 1)], own_send)
    wait_bytes(series.at[pl.ds(0, (groups - 1) * piece)], first_send)
    wait_bytes(scales.at[pl.ds(0, groups - 1)], scale_send)
    wait_bytes(chosen.at[:, :, pl.ds(0, flat - 1)], second_send)
    wait_bytes(full.at[:, pl.ds(0, 3)], y_send)
    wait_bytes(full.at[:, pl.ds(0, 4)], core_send)


def on_device(sizes, series, partner):
    Z, YL, X, YH, C = sizes
    groups, flat, quarters = Z * YL * X, Z * X, YH * C
    points, days = series.shape
    piece, rows, span = points // groups, points // quarters, days // CHUNKS
    bf16 = jnp.bfloat16
    dma = pltpu.SemaphoreType.DMA
    total = pl.pallas_call(
        functools.partial(kernel, sizes),
        out_shape=jax.ShapeDtypeStruct((rows, points), jnp.float32),
        in_specs=[
            pl.BlockSpec(memory_space=pltpu.SMEM),
            pl.BlockSpec(memory_space=pl.ANY),
        ],
        out_specs=pl.BlockSpec(memory_space=pltpu.VMEM),
        scratch_shapes=[
            pltpu.VMEM((points, days), bf16),
            pltpu.VMEM((quarters, points // 128, 2, 128), jnp.float32),
            pltpu.VMEM((points // 128, 2, 128), jnp.float32),
            pltpu.VMEM((groups, 2, 128), jnp.float32),
            pltpu.VMEM((groups, piece, 128), jnp.float32),
            pltpu.VMEM((groups, piece, 128), jnp.float32),
            [pltpu.VMEM((groups, piece, days // FIRST_PARTS), bf16) for _ in range(FIRST_PARTS)],
            pltpu.VMEM((CHUNKS, YL, flat, piece, span), bf16),
            pltpu.VMEM((CHUNKS, YL, flat, piece, span), bf16),
            pltpu.VMEM((quarters, rows, days), bf16),
            pltpu.VMEM((CHUNKS, YL * quarters, flat, piece, span), bf16),
            pltpu.SemaphoreType.REGULAR,
            dma,
            dma,
            dma((quarters - 1,)),
            dma,
            dma,
            dma,
            dma,
            dma,
            dma((FIRST_PARTS,)),
            dma,
            dma((2 * CHUNKS,)),
            dma,
            dma((CHUNKS, 3)),
            dma,
            dma((CHUNKS,)),
        ],
        compiler_params=pltpu.CompilerParams(
            collective_id=0, has_side_effects=True, vmem_limit_bytes=46 * 2**20
        ),
        cost_estimate=pl.CostEstimate(
            flops=2 * rows * points * days * quarters, bytes_accessed=12 * 2**20, transcendentals=0
        ),
    )(partner, series)
    correlation = total * (1.0 / (days * quarters))
    degree = jnp.sum(correlation * correlation, axis=1)
    return (correlation, degree)


def solution(mesh):
    sizes = (8, 2, 4, 2, 2)
    fine = Mesh(mesh.devices.reshape(sizes), PTS + DAYS)
    in_specs = (P(PTS, DAYS), P())
    out_specs = (P(PTS + DAYS, None), P(PTS + DAYS))
    return jax.shard_map(
        functools.partial(on_device, sizes), mesh=fine, in_specs=in_specs, out_specs=out_specs, check_vma=False
    )
```

time: 244 us -> 214 us (0.88)
  Pallas kernels: 238 us -> 209 us
    pallas_call x1, Pallas kernels: 238 us -> 209 us  [on_device(): pl.pallas_call(functools.partial(kernel, sizes), out_shape=jax.ShapeDtype...]
where the time goes in v2:
time: 214 us; the launch traced here: 213 us
  Pallas kernels  209 us (98%)
  other arithmetic  2.99 us (1%)
    pallas_call x1, Pallas kernels, on_device(): pl.pallas_call(functools.partial(kernel, sizes), out_shape=jax.ShapeDtype...  209 us

profile of v2, /device:TPU:1, one launch (start us, length us, event | category | flops | bytes accessed | tf_op | source)
XLA Modules:
  0.0 213.4 jit_solution(15071573021872607763)
XLA Ops:
  0.6 0.0 copy-start
  0.6 0.6 copy-done
  1.3 209.1 %shard_map.41 = f32[512,2048]{1,0:T(8,128)S(1)} custom-call(s32[64]{0:T(128)S(1)} %copy-done, bf16[2048,1024]{1,0:T(8,128)(2,1)} %series.1), custom_call_target="tpu_custom_call" | custom-call | flops 8589934592 | bytes 12582912 | tf_op jit(solution)/shard_map/pallas_call | solution.py:345
  210.4 3.0 %multiply_reduce_fusion = (f32[512]{0:T(512)}, f32[512,2048]{1,0:T(8,128)}) fusion(f32[512,2048]{1,0:T(8,128)S(1)} %shard_map.41), kind=kLoop, calls=%fused_computation | loop fusion | flops 3145216 | bytes 8390656 | tf_op jit(solution)/shard_map/reduce_sum | solution.py:390
Async XLA Ops:
  0.6 0.7 copy-start

commit v3 on v2

--- a/solution.py
+++ b/solution.py
@@ -13,8 +13,9 @@
 DAYS = ("yh", "core")
 FIRST_PARTS = 4
 CHUNKS = 8
-AHEAD = 3
-LAG = 2
+SPLIT = 2
+AHEAD = 4
+LAG = 3
 MESH = pl.DeviceIdType.MESH
 
 
@@ -109,9 +110,8 @@
     pl.semaphore_wait(barrier, plane - 1 + Z - 1 + quarters - 1 + 1)
     for o in range(1, plane):
         pl.semaphore_signal(gate, inc=1, device_id=plane_peer(o), device_id_type=MESH)
-    pl.semaphore_wait(gate, plane - 1)
-
-    def first_part(part):
+
+    def first_part(part, low, high):
         cols = pl.ds(part * width, width)
 
         def send(o, carry):
@@ -128,9 +128,11 @@
             ).start()
             return carry
 
-        lax.fori_loop(1, groups, send, 0)
-
-    first_part(0)
+        lax.fori_loop(low, high, send, 0)
+
+    first_part(0, 1, Z)
+    pl.semaphore_wait(gate, plane - 1)
+    first_part(0, Z, groups)
     local_copy.wait()
 
     eye = lax.broadcasted_iota(jnp.int32, (tile, tile), 0) == lax.broadcasted_iota(jnp.int32, (tile, tile), 1)
@@ -155,7 +157,7 @@
         _, ph, pc = other_day(o)
         remote(stats.at[day], stats.at[day], stat_send, stat_recv.at[o - 1], yh=ph, core=pc).start()
     if FIRST_PARTS > 1:
-        first_part(1)
+        first_part(1, 1, groups)
     for o in range(1, quarters):
         wait_bytes(stats.at[0], stat_recv.at[o - 1])
 
@@ -190,7 +192,7 @@
             core=pc,
         ).start()
     for part in range(2, FIRST_PARTS):
-        first_part(part)
+        first_part(part, 1, groups)
     for part in range(FIRST_PARTS):
         cols = pl.ds(part * width, width)
         inboxes[part][block] = local[pl.ds(pl.multiple_of(mine * piece, piece), piece), cols]
@@ -222,30 +224,35 @@
 
         lax.fori_loop(0, rows // tile, one, 0)
 
-    def half_of(unit):
-        return 1 - yl if unit % 2 else yl
+    thin = piece // SPLIT
+    per_chunk = 2 * SPLIT
+
+    def parts_of(unit):
+        k, rest = unit // per_chunk, unit % per_chunk
+        rel, r = rest // SPLIT, rest % SPLIT
+        return k, rel, r, 1 - yl if rel else yl, pl.ds(r * thin, thin)
 
     def second_hop(unit):
-        k, half = unit // 2, half_of(unit)
+        k, _, _, half, lines = parts_of(unit)
         inbox = inboxes[k * span // width]
 
         def pick(t, carry):
             source = partner[(t // X * YL + half) * X + lax.rem(t, X)]
             for j in range(0, span, tile):
-                values = inbox[source, :, pl.ds(k * span % width + j, tile)].astype(jnp.float32)
-                values = (values - shift[source]) * factor[source]
-                chosen[k, half, t, :, pl.ds(j, tile)] = values.astype(jnp.bfloat16)
+                values = inbox[source, lines, pl.ds(k * span % width + j, tile)].astype(jnp.float32)
+                values = (values - shift[source, lines]) * factor[source, lines]
+                chosen[k, half, t, lines, pl.ds(j, tile)] = values.astype(jnp.bfloat16)
             return carry
 
         lax.fori_loop(0, flat, pick, 0)
-        landed[k, half, zx] = chosen[k, half, zx]
+        landed[k, half, zx, lines] = chosen[k, half, zx, lines]
 
         def send(o, carry):
             pz = lax.rem(z + lax.rem(o * 3, Z), Z)
             px = lax.rem(x + o // Z, X)
             remote(
-                chosen.at[k, half, pz * X + px],
-                landed.at[k, half, zx],
+                chosen.at[k, half, pz * X + px, lines],
+                landed.at[k, half, zx, lines],
                 second_send,
                 second_recv.at[unit],
                 z=pz,
@@ -256,37 +263,37 @@
         lax.fori_loop(1, flat, send, 0)
 
     def spread_y(unit):
-        k, half = unit // 2, half_of(unit)
-        wait_bytes(chosen.at[k, 0, pl.ds(0, flat - 1)], second_recv.at[unit])
-        if unit % 2 == 0:
-            remote(landed.at[k, half], full.at[k, here], y_send, y_recv.at[k, 0], yh=1 - yh).start()
-            remote(landed.at[k, half], full.at[k, here], core_send, core_recv.at[k], core=1 - core).start()
-            full[k, here] = landed[k, half]
+        k, rel, r, half, lines = parts_of(unit)
+        wait_bytes(chosen.at[k, 0, pl.ds(0, flat - 1), lines], second_recv.at[unit])
+        source, target = landed.at[k, half, :, lines], full.at[k, here, :, lines]
+        if rel == 0:
+            remote(source, target, y_send, y_recv.at[k, 0, r], yh=1 - yh).start()
+            remote(source, target, core_send, core_recv.at[k, 0], core=1 - core).start()
+            full[k, here, :, lines] = landed[k, half, :, lines]
         else:
             for to in range(YH):
-                remote(
-                    landed.at[k, half], full.at[k, here], y_send, y_recv.at[k, 1 + yh], yl=1 - yl, yh=to
-                ).start()
+                remote(source, target, y_send, y_recv.at[k, 1 + yh, r], yl=1 - yl, yh=to).start()
 
     def spread_core(unit):
-        k = unit // 2
-        if unit % 2 == 0:
+        k, rel, r, _, lines = parts_of(unit)
+        if rel == 0:
             arrivals = [(0, yl * quarters + (1 - yh) * C + core)]
         else:
             arrivals = [(1 + h, (1 - yl) * quarters + h * C + core) for h in range(YH)]
         for j, at in arrivals:
-            wait_bytes(full.at[k, 0], y_recv.at[k, j])
-            remote(full.at[k, at], full.at[k, at], core_send, core_recv.at[k], core=1 - core).start()
+            wait_bytes(full.at[k, 0, :, lines], y_recv.at[k, j, r])
+            remote(
+                full.at[k, at, :, lines], full.at[k, at, :, lines], core_send, core_recv.at[k, rel], core=1 - core
+            ).start()
 
     columns = min(256, flat * piece)
     tiles = flat * piece // columns
 
-    def multiply(k, cores):
+    def multiply(k, half, cores):
         quarter = [h * C + c for c in cores for h in range(YH)]
         group = columns // piece
 
-        def one(n, carry):
-            half, t = n // tiles, lax.rem(n, tiles)
+        def one(t, carry):
             left = jnp.concatenate([own[q, :, pl.ds(k * span, span)] for q in quarter], axis=1)
             right = jnp.concatenate(
                 [
@@ -296,17 +303,18 @@
                 axis=1,
             )
             total = lax.dot_general(left, right, (((1,), (1,)), ((), ())), preferred_element_type=jnp.float32)
-            at = pl.ds(pl.multiple_of(n * columns, columns), columns)
+            at = pl.ds(pl.multiple_of((half * tiles + t) * columns, columns), columns)
             out[:, at] = total if k == 0 else out[:, at] + total
             return carry
 
-        lax.fori_loop(0, YL * tiles, one, 0)
-
-    units = 2 * CHUNKS
+        lax.fori_loop(0, tiles, one, 0)
+
+    units = per_chunk * CHUNKS
     for step in range(units + AHEAD + LAG + 1):
         if step < units:
-            if step // 2 * span % width == 0 and step % 2 == 0:
-                part = step // 2 * span // width
+            k = step // per_chunk
+            if step % per_chunk == 0 and k * span % width == 0:
+                part = k * span // width
                 wait_bytes(inboxes[part].at[pl.ds(0, groups - 1)], first_recv.at[part])
             second_hop(step)
         unit = step - AHEAD
@@ -316,15 +324,16 @@
         if 0 <= unit < units:
             spread_core(unit)
         unit = step - AHEAD - LAG - 1
-        if unit > 0 and unit % 2:
-            k = unit // 2
-            if k == 0:
+        if unit >= 0 and unit % SPLIT == SPLIT - 1:
+            k, rel, _, half, _ = parts_of(unit)
+            last = unit == units - 1
+            if k == 0 and rel == 0:
                 wait_bytes(own.at[pl.ds(0, quarters - 1)], own_recv)
                 normalise_own()
-            if k == CHUNKS - 1:
-                multiply(k, [core])
-            wait_bytes(full.at[k, pl.ds(0, 4)], core_recv.at[k])
-            multiply(k, [1 - core] if k == CHUNKS - 1 else range(C))
+            if last:
+                multiply(k, half, [core])
+            wait_bytes(full.at[k, pl.ds(0, 2)], core_recv.at[k, rel])
+            multiply(k, half, [1 - core] if last else range(C))
 
     wait_bytes(stats.at[pl.ds(0, quarters - 1)], stat_send)
     wait_bytes(own.at[pl.ds(0, quarters - 1)], own_send)
@@ -373,11 +382,11 @@
             dma,
             dma((FIRST_PARTS,)),
             dma,
-            dma((2 * CHUNKS,)),
-            dma,
-            dma((CHUNKS, 3)),
-            dma,
-            dma((CHUNKS,)),
+            dma((2 * SPLIT * CHUNKS,)),
+            dma,
+            dma((CHUNKS, 3, SPLIT)),
+            dma,
+            dma((CHUNKS, 2)),
         ],
         compiler_params=pltpu.CompilerParams(
             collective_id=0, has_side_effects=True, vmem_limit_bytes=46 * 2**20

time: 214 us -> 210 us (0.981)
  Pallas kernels: 209 us -> 205 us
    pallas_call x1, Pallas kernels: 209 us -> 205 us  [on_device(): pl.pallas_call(functools.partial(kernel, sizes), out_shape=jax.ShapeDtype...]
where the time goes in v3:
time: 210 us
  Pallas kernels  205 us (98%)
  other arithmetic  2.99 us (1%)
    pallas_call x1, Pallas kernels, on_device(): pl.pallas_call(functools.partial(kernel, sizes), out_shape=jax.ShapeDtype...  205 us

profile of v3, /device:TPU:1, one launch (start us, length us, event | category | flops | bytes accessed | tf_op | source)
XLA Modules:
  0.0 209.7 jit_solution(18242084293049283676)
XLA Ops:
  0.6 0.0 copy-start
  0.6 0.6 copy-done
  1.3 205.5 %shard_map.41 = f32[512,2048]{1,0:T(8,128)S(1)} custom-call(s32[64]{0:T(128)S(1)} %copy-done, bf16[2048,1024]{1,0:T(8,128)(2,1)} %series.1), custom_call_target="tpu_custom_call" | custom-call | flops 8589934592 | bytes 12582912 | tf_op jit(solution)/shard_map/pallas_call | solution.py:354
  206.8 3.0 %multiply_reduce_fusion = (f32[512]{0:T(512)}, f32[512,2048]{1,0:T(8,128)}) fusion(f32[512,2048]{1,0:T(8,128)S(1)} %shard_map.41), kind=kLoop, calls=%fused_computation | loop fusion | flops 3145216 | bytes 8390656 | tf_op jit(solution)/shard_map/reduce_sum | solution.py:399
Async XLA Ops:
  0.6 0.7 copy-start

commit v4 on v3

--- a/solution.py
+++ b/solution.py
@@ -133,54 +133,6 @@
     first_part(0, 1, Z)
     pl.semaphore_wait(gate, plane - 1)
     first_part(0, Z, groups)
-    local_copy.wait()
-
-    eye = lax.broadcasted_iota(jnp.int32, (tile, tile), 0) == lax.broadcasted_iota(jnp.int32, (tile, tile), 1)
-
-    def to_lanes(column):
-        return jnp.sum(jnp.where(eye, column, 0.0), axis=0, keepdims=True)
-
-    def to_rows(line):
-        return jnp.sum(jnp.where(eye, line, 0.0), axis=1, keepdims=True)
-
-    def local_stats(g, carry):
-        values = local[pl.ds(pl.multiple_of(g * tile, tile), tile), :].astype(jnp.float32)
-        mean = jnp.sum(values, axis=1, keepdims=True) / days
-        centred = values - mean
-        squares = jnp.sum(centred * centred, axis=1, keepdims=True)
-        stats[day, g, pl.ds(0, 1), :] = to_lanes(mean)
-        stats[day, g, pl.ds(1, 1), :] = to_lanes(squares)
-        return carry
-
-    lax.fori_loop(0, points // tile, local_stats, 0)
-    for o in range(1, quarters):
-        _, ph, pc = other_day(o)
-        remote(stats.at[day], stats.at[day], stat_send, stat_recv.at[o - 1], yh=ph, core=pc).start()
-    if FIRST_PARTS > 1:
-        first_part(1, 1, groups)
-    for o in range(1, quarters):
-        wait_bytes(stats.at[0], stat_recv.at[o - 1])
-
-    def whole_stats(g, carry):
-        means = [stats[d, g, pl.ds(0, 1), :] for d in range(quarters)]
-        average = sum(means) / quarters
-        spread = sum(stats[d, g, pl.ds(1, 1), :] for d in range(quarters))
-        spread += days * sum((m - average) * (m - average) for m in means)
-        final[g, pl.ds(0, 1), :] = average
-        final[g, pl.ds(1, 1), :] = lax.rsqrt(spread / (days * quarters) + epsilon)
-        return carry
-
-    lax.fori_loop(0, points // tile, whole_stats, 0)
-
-    def send_scale(o, carry):
-        pz, py, px = peer(o)
-        to = py * flat + pz * X + px
-        remote(
-            final.at[to // per_tile], scales.at[block], scale_send, scale_recv, z=pz, yl=py, x=px
-        ).start()
-        return carry
-
-    lax.fori_loop(1, groups, send_scale, 0)
     for o in range(1, quarters):
         to, ph, pc = other_day(o)
         remote(
@@ -191,6 +143,54 @@
             yh=ph,
             core=pc,
         ).start()
+    local_copy.wait()
+
+    eye = lax.broadcasted_iota(jnp.int32, (tile, tile), 0) == lax.broadcasted_iota(jnp.int32, (tile, tile), 1)
+
+    def to_lanes(column):
+        return jnp.sum(jnp.where(eye, column, 0.0), axis=0, keepdims=True)
+
+    def to_rows(line):
+        return jnp.sum(jnp.where(eye, line, 0.0), axis=1, keepdims=True)
+
+    def local_stats(g, carry):
+        values = local[pl.ds(pl.multiple_of(g * tile, tile), tile), :].astype(jnp.float32)
+        mean = jnp.sum(values, axis=1, keepdims=True) / days
+        centred = values - mean
+        squares = jnp.sum(centred * centred, axis=1, keepdims=True)
+        stats[day, g, pl.ds(0, 1), :] = to_lanes(mean)
+        stats[day, g, pl.ds(1, 1), :] = to_lanes(squares)
+        return carry
+
+    lax.fori_loop(0, points // tile, local_stats, 0)
+    for o in range(1, quarters):
+        _, ph, pc = other_day(o)
+        remote(stats.at[day], stats.at[day], stat_send, stat_recv.at[o - 1], yh=ph, core=pc).start()
+    if FIRST_PARTS > 1:
+        first_part(1, 1, groups)
+    for o in range(1, quarters):
+        wait_bytes(stats.at[0], stat_recv.at[o - 1])
+
+    def whole_stats(g, carry):
+        means = [stats[d, g, pl.ds(0, 1), :] for d in range(quarters)]
+        average = sum(means) / quarters
+        spread = sum(stats[d, g, pl.ds(1, 1), :] for d in range(quarters))
+        spread += days * sum((m - average) * (m - average) for m in means)
+        final[g, pl.ds(0, 1), :] = average
+        final[g, pl.ds(1, 1), :] = lax.rsqrt(spread / (days * quarters) + epsilon)
+        return carry
+
+    lax.fori_loop(0, points // tile, whole_stats, 0)
+
+    def send_scale(o, carry):
+        pz, py, px = peer(o)
+        to = py * flat + pz * X + px
+        remote(
+            final.at[to // per_tile], scales.at[block], scale_send, scale_recv, z=pz, yl=py, x=px
+        ).start()
+        return carry
+
+    lax.fori_loop(1, groups, send_scale, 0)
     for part in range(2, FIRST_PARTS):
         first_part(part, 1, groups)
     for part in range(FIRST_PARTS):

time: 210 us -> 241 us (1.15)
  Pallas kernels: 205 us -> 237 us
    pallas_call x1, Pallas kernels: 205 us -> 237 us  [on_device(): pl.pallas_call(functools.partial(kernel, sizes), out_shape=jax.ShapeDtype...]
where the time goes in v4:
time: 241 us
  Pallas kernels  237 us (98%)
  other arithmetic  2.99 us (1%)
    pallas_call x1, Pallas kernels, on_device(): pl.pallas_call(functools.partial(kernel, sizes), out_shape=jax.ShapeDtype...  237 us

profile of v4, /device:TPU:1, one launch (start us, length us, event | category | flops | bytes accessed | tf_op | source)
XLA Modules:
  0.0 241.0 jit_solution(14018621740210480753)
XLA Ops:
  0.6 0.0 copy-start
  0.6 0.6 copy-done
  1.3 236.7 %shard_map.41 = f32[512,2048]{1,0:T(8,128)S(1)} custom-call(s32[64]{0:T(128)S(1)} %copy-done, bf16[2048,1024]{1,0:T(8,128)(2,1)} %series.1), custom_call_target="tpu_custom_call" | custom-call | flops 8589934592 | bytes 12582912 | tf_op jit(solution)/shard_map/pallas_call | solution.py:354
  238.0 3.0 %multiply_reduce_fusion = (f32[512]{0:T(512)}, f32[512,2048]{1,0:T(8,128)}) fusion(f32[512,2048]{1,0:T(8,128)S(1)} %shard_map.41), kind=kLoop, calls=%fused_computation | loop fusion | flops 3145216 | bytes 8390656 | tf_op jit(solution)/shard_map/reduce_sum | solution.py:399
Async XLA Ops:
  0.6 0.7 copy-start
